TPU v7x, 512 devices: a whole 4x8x8 slice. The times are simulated.
512 devices in a mesh: gx: 16 (over y, z_hi), gy: 32 (over z_lo, x, core).
Axes of the slice: x: 4, y: 8, z: 8 (z_hi: 2, z_lo: 4; z = z_hi * 4 + z_lo), core: 2. Of those that a mesh axis runs over, the one named last changes fastest.
Arguments:
- images: float32 [131072, 1152], P(('gx', 'gy')), may hold values from -0.17677669 to 0.17677669
- texts: float32 [131072, 1152], P(('gx', 'gy')), may hold values from -0.17677669 to 0.17677669
- log_temp: float32 [1], replicated, may hold values from 1.6 to 3
- bias: float32 [1], replicated, may hold values from -3 to -1
Outputs:
- row_loss: float32 [131072], P(('gx', 'gy'))
- image_grad: float32 [131072, 1152], P(('gx', 'gy'))
- text_grad: float32 [131072, 1152], P(('gx', 'gy'))
All inputs are finite; a program needn't handle non-finite values.
Results may differ from a plain program's by a relative error of at most 0.00011.
Values sent between devices are 32-bit elements; how exact they have to be, the bound alone decides.
A program may use at most 64 MiB of HBM per device.

v0:
```python
import jax
import jax.numpy as jnp
from jax import lax
from jax.sharding import PartitionSpec as P

STEPS = 4


def from_behind(block, axis, distance):
    devices = range(lax.axis_size(axis))
    route = [((i - distance) % len(devices), i) for i in devices]
    return lax.ppermute(block, axis, route)


def per_device(images, texts, log_temp, bias):
    rows = images.shape[0]
    temp = jnp.exp(log_temp[0])
    shift_b = bias[0]
    eye = jnp.eye(rows, dtype=jnp.float32)
    highest = lax.Precision.HIGHEST

    def pair_block(partner, first):
        logits = (
            temp * lax.dot_general(images, partner, (((1,), (1,)), ((), ())), precision=highest)
            + shift_b
        )
        if first:
            signs = 2.0 * eye - 1.0
            coeff = jax.nn.sigmoid(logits) - eye
        else:
            signs = -1.0
            coeff = jax.nn.sigmoid(logits)
        losses = jnp.sum(jax.nn.softplus(-signs * logits), axis=1)
        img_part = temp * jnp.dot(coeff, partner, precision=highest)
        txt_part = temp * lax.dot_general(
            coeff, images, (((0,), (0,)), ((), ())), precision=highest
        )
        return (losses, img_part, txt_part)

    row_sum, image_grad, text_grad = pair_block(texts, True)
    partner = texts
    carried = text_grad
    for step in range(1, STEPS):
        partner, carried = from_behind((partner, carried), ("gx", "gy"), 1)
        losses, img_part, txt_part = pair_block(partner, False)
        row_sum = row_sum + losses
        image_grad = image_grad + img_part
        carried = carried + txt_part
    text_grad = from_behind(carried, ("gx", "gy"), 1 - STEPS)
    row_loss = row_sum / (STEPS * rows)
    return (row_loss, image_grad, text_grad)


def solution(mesh):
    return jax.shard_map(
        per_device,
        mesh=mesh,
        in_specs=(P(("gx", "gy"), None), P(("gx", "gy"), None), P(), P()),
        out_specs=(P(("gx", "gy")), P(("gx", "gy"), None), P(("gx", "gy"), None)),
        check_vma=False,
    )
```

profile of v0, /device:TPU:1, one launch (start us, length us, event | category | flops | bytes accessed | tf_op | source)
XLA Modules:
  0.0 125.2 jit_solution(9809944359849497695)
XLA Ops:
  0.6 0.0 copy-start
  0.6 4.6 %collective-permute-start = (f32[256,1152]{1,0:T(8,128)}, f32[256,1152]{1,0:T(8,128)S(1)}, u32[]{:S(2)}, u32[]{:S(2)}) collective-permute-start(f32[256,1152]{1,0:T(8,128)} %param.5), channel_id=1, source_target_pairs={{511,0},{0,1},{1,2},{2,3},{3,4},{4,5},{5,6},{6,7},{7,8},{8,9},{9,1... | collective-permute-start | bytes 3538952 | tf_op jit(solution)/shard_map/ppermute | solution.py:12
  6.6 2.7 %fusion.6 = (f32[256]{0:T(256)S(1)}, f32[256,256]{0,1:T(8,128)S(1)}) fusion(f32[]{:T(128)} %bitcast.18, f32[256,1152]{1,0:T(8,128)S(1)} %copy-done, f32[256,1152]{1,0:T(8,128)} %param.5, f32[]{:T(128)} %bitcast), kind=kOutput, calls=%fused_computation.21 | convolution fusion | flops 906886912 | bytes 2622472 | tf_op jit(solution)/shard_map/dot_general | solution.py:24
  9.3 1.3 %convolution_multiply_fusion.3 = f32[256,1152]{1,0:T(8,128)S(1)} fusion(f32[256,1152]{1,0:T(8,128)S(1)} %copy-done, f32[]{:T(128)} %bitcast, f32[256,256]{0,1:T(8,128)S(1)} %get-tuple-element.8), kind=kOutput, calls=%fused_computation.4 | convolution fusion | flops 906657792 | bytes 2621444 | tf_op jit(solution)/shard_map/dot_general | solution.py:35
  10.6 1.9 %collective-permute-start.3 = (f32[256,1152]{1,0:T(8,128)S(1)}, f32[256,1152]{1,0:T(8,128)S(1)}, u32[]{:S(2)}, u32[]{:S(2)}) collective-permute-start(f32[256,1152]{1,0:T(8,128)S(1)} %convolution_multiply_fusion.3), channel_id=1, source_target_pairs={{511,0},{0,1},{1,2},{2,3},{3,4},{4,5},{5,6},{6,7},{7,8},{8,9},{9,1... | collective-permute-start | bytes 3538952 | tf_op jit(solution)/shard_map/ppermute | solution.py:12
  12.6 6.2 %collective-permute-done = f32[256,1152]{1,0:T(8,128)S(1)} collective-permute-done((f32[256,1152]{1,0:T(8,128)}, f32[256,1152]{1,0:T(8,128)S(1)}, u32[]{:S(2)}, u32[]{:S(2)}) %collective-permute-start) | collective-permute-done | bytes 1179680 | tf_op jit(solution)/shard_map/ppermute | solution.py:12
  18.7 4.3 %collective-permute-start.1 = (f32[256,1152]{1,0:T(8,128)S(1)}, f32[256,1152]{1,0:T(8,128)S(1)}, u32[]{:S(2)}, u32[]{:S(2)}) collective-permute-start(f32[256,1152]{1,0:T(8,128)S(1)} %collective-permute-done), channel_id=1, source_target_pairs={{511,0},{0,1},{1,2},{2,3},{3,4},{4,5},{5,6},{6,7},{7,8},{8,9},{9,1... | collective-permute-start | bytes 3538952 | tf_op jit(solution)/shard_map/ppermute | solution.py:12
  23.0 1.4 %fusion.7 = (f32[256]{0:T(256)S(1)}, f32[256,256]{0,1:T(8,128)S(1)}) fusion(f32[]{:T(128)} %bitcast.21, f32[256,1152]{1,0:T(8,128)S(1)} %copy-done, f32[256,1152]{1,0:T(8,128)S(1)} %collective-permute-done, f32[]{:T(128)} %bitcast), kind=kOutput, calls=%fused_computation.22 | convolution fusion | flops 906559232 | bytes 2622472 | tf_op jit(solution)/shard_map/dot_general | solution.py:24
  24.4 6.9 %collective-permute-done.3 = f32[256,1152]{1,0:T(8,128)S(1)} collective-permute-done((f32[256,1152]{1,0:T(8,128)S(1)}, f32[256,1152]{1,0:T(8,128)S(1)}, u32[]{:S(2)}, u32[]{:S(2)}) %collective-permute-start.3) | collective-permute-done | bytes 1179680 | tf_op jit(solution)/shard_map/ppermute | solution.py:12
  31.3 1.3 %fusion = f32[256,1152]{1,0:T(8,128)S(1)} fusion(f32[256,1152]{1,0:T(8,128)S(1)} %collective-permute-done.3, f32[256,1152]{1,0:T(8,128)S(1)} %copy-done, f32[]{:T(128)} %bitcast, f32[256,256]{0,1:T(8,128)S(1)} %get-tuple-element.10), kind=kOutput, calls=%fused_computation.3 | convolution fusion | flops 906756096 | bytes 3801092 | tf_op jit(solution)/shard_map/dot_general | solution.py:35
  32.6 4.4 %collective-permute-start.4 = (f32[256,1152]{1,0:T(8,128)S(1)}, f32[256,1152]{1,0:T(8,128)S(1)}, u32[]{:S(2)}, u32[]{:S(2)}) collective-permute-start(f32[256,1152]{1,0:T(8,128)S(1)} %fusion), channel_id=1, source_target_pairs={{511,0},{0,1},{1,2},{2,3},{3,4},{4,5},{5,6},{6,7},{7,8},{8,9},{9,1... | collective-permute-start | bytes 3538952 | tf_op jit(solution)/shard_map/ppermute | solution.py:12
  37.0 6.9 %collective-permute-done.1 = f32[256,1152]{1,0:T(8,128)S(1)} collective-permute-done((f32[256,1152]{1,0:T(8,128)S(1)}, f32[256,1152]{1,0:T(8,128)S(1)}, u32[]{:S(2)}, u32[]{:S(2)}) %collective-permute-start.1) | collective-permute-done | bytes 1179680 | tf_op jit(solution)/shard_map/ppermute | solution.py:12
  43.9 4.4 %collective-permute-start.2 = (f32[256,1152]{1,0:T(8,128)S(1)}, f32[256,1152]{1,0:T(8,128)S(1)}, u32[]{:S(2)}, u32[]{:S(2)}) collective-permute-start(f32[256,1152]{1,0:T(8,128)S(1)} %collective-permute-done.1), channel_id=1, source_target_pairs={{511,0},{0,1},{1,2},{2,3},{3,4},{4,5},{5,6},{6,7},{7,8},{8,9},{9,1... | collective-permute-start | bytes 3538952 | tf_op jit(solution)/shard_map/ppermute | solution.py:12
  48.3 1.4 %fusion.8 = (f32[256]{0:T(256)S(1)}, f32[256,256]{0,1:T(8,128)S(1)}) fusion(f32[]{:T(128)} %bitcast.20, f32[256,1152]{1,0:T(8,128)S(1)} %copy-done, f32[256,1152]{1,0:T(8,128)S(1)} %collective-permute-done.1, f32[]{:T(128)} %bitcast), kind=kOutput, calls=%fused_computation.23 | convolution fusion | flops 906559232 | bytes 2622472 | tf_op jit(solution)/shard_map/dot_general | solution.py:24
  49.7 1.3 %convolution_multiply_fusion.1 = f32[256,1152]{1,0:T(8,128)S(1)} fusion(f32[256,1152]{1,0:T(8,128)S(1)} %copy-done, f32[]{:T(128)} %bitcast, f32[256,256]{0,1:T(8,128)S(1)} %get-tuple-element.6), kind=kOutput, calls=%fused_computation.1 | convolution fusion | flops 906461184 | bytes 2621444 | tf_op jit(solution)/shard_map/dot_general | solution.py:35
  51.0 0.0 copy-start.1
  51.0 5.6 %collective-permute-done.4 = f32[256,1152]{1,0:T(8,128)S(1)} collective-permute-done((f32[256,1152]{1,0:T(8,128)S(1)}, f32[256,1152]{1,0:T(8,128)S(1)}, u32[]{:S(2)}, u32[]{:S(2)}) %collective-permute-start.4) | collective-permute-done | bytes 1179680 | tf_op jit(solution)/shard_map/ppermute | solution.py:12
  56.6 0.1 add.91
  56.7 4.6 %collective-permute-start.5 = (f32[256,1152]{1,0:T(8,128)S(1)}, f32[256,1152]{1,0:T(8,128)S(1)}, u32[]{:S(2)}, u32[]{:S(2)}) collective-permute-start(f32[256,1152]{1,0:T(8,128)S(1)} %add.91), channel_id=1, source_target_pairs={{511,0},{0,1},{1,2},{2,3},{3,4},{4,5},{5,6},{6,7},{7,8},{8,9},{9,1... | collective-permute-start | bytes 3538952 | tf_op jit(solution)/shard_map/ppermute | solution.py:12
  61.3 1.3 %fusion.10 = f32[256,1152]{1,0:T(8,128)S(1)} fusion(f32[256,1152]{1,0:T(8,128)S(1)} %copy-done.1, f32[256,256]{0,1:T(8,128)S(1)} %get-tuple-element.8), kind=kOutput, calls=%fused_computation.30 | convolution fusion | flops 906362880 | bytes 2621440 | tf_op jit(solution)/shard_map/dot_general | solution.py:34
  62.5 6.6 %collective-permute-done.2 = f32[256,1152]{1,0:T(8,128)S(1)} collective-permute-done((f32[256,1152]{1,0:T(8,128)S(1)}, f32[256,1152]{1,0:T(8,128)S(1)}, u32[]{:S(2)}, u32[]{:S(2)}) %collective-permute-start.2) | collective-permute-done | bytes 1179680 | tf_op jit(solution)/shard_map/ppermute | solution.py:12
  69.2 1.4 %fusion.9 = (f32[256]{0:T(256)S(1)}, f32[256,256]{0,1:T(8,128)S(1)}) fusion(f32[]{:T(128)} %bitcast.19, f32[256,1152]{1,0:T(8,128)S(1)} %copy-done, f32[256,1152]{1,0:T(8,128)S(1)} %collective-permute-done.2, f32[]{:T(128)} %bitcast), kind=kOutput, calls=%fused_computation.24 | convolution fusion | flops 906559232 | bytes 2622472 | tf_op jit(solution)/shard_map/dot_general | solution.py:24
  70.6 1.3 %convolution_multiply_fusion = f32[256,1152]{1,0:T(8,128)S(1)} fusion(f32[256,1152]{1,0:T(8,128)S(1)} %copy-done, f32[]{:T(128)} %bitcast, f32[256,256]{0,1:T(8,128)S(1)} %get-tuple-element.4), kind=kOutput, calls=%fused_computation | convolution fusion | flops 906461184 | bytes 2621444 | tf_op jit(solution)/shard_map/dot_general | solution.py:35
  71.9 10.0 %collective-permute-done.5 = f32[256,1152]{1,0:T(8,128)S(1)} collective-permute-done((f32[256,1152]{1,0:T(8,128)S(1)}, f32[256,1152]{1,0:T(8,128)S(1)}, u32[]{:S(2)}, u32[]{:S(2)}) %collective-permute-start.5) | collective-permute-done | bytes 1179680 | tf_op jit(solution)/shard_map/ppermute | solution.py:12
  81.8 0.1 add.92
  82.0 17.0 %collective-permute-start.6 = (f32[256,1152]{1,0:T(8,128)S(1)}, f32[256,1152]{1,0:T(8,128)S(1)}, u32[]{:S(2)}, u32[]{:S(2)}) collective-permute-start(f32[256,1152]{1,0:T(8,128)S(1)} %add.92), channel_id=1, source_target_pairs={{3,0},{4,1},{5,2},{6,3},{7,4},{8,5},{9,6},{10,7},{11,8},{12,9},{13... | collective-permute-start | bytes 3538952 | tf_op jit(solution)/shard_map/ppermute | solution.py:12
  99.0 1.3 %convolution_add_fusion.2 = f32[256,1152]{1,0:T(8,128)S(1)} fusion(f32[256,1152]{1,0:T(8,128)S(1)} %fusion.10, f32[256,1152]{1,0:T(8,128)S(1)} %collective-permute-done, f32[256,256]{0,1:T(8,128)S(1)} %get-tuple-element.10), kind=kOutput, calls=%fused_computation.8 | convolution fusion | flops 906461184 | bytes 3801088 | tf_op jit(solution)/shard_map/dot_general | solution.py:34
  100.3 1.3 %convolution_add_fusion.1 = f32[256,1152]{1,0:T(8,128)S(1)} fusion(f32[256,1152]{1,0:T(8,128)S(1)} %convolution_add_fusion.2, f32[256,1152]{1,0:T(8,128)S(1)} %collective-permute-done.1, f32[256,256]{0,1:T(8,128)S(1)} %get-tuple-element.6), kind=kOutput, calls=%fused_computation.7 | convolution fusion | flops 906461184 | bytes 3801088 | tf_op jit(solution)/shard_map/dot_general | solution.py:34
  101.6 0.6 add_multiply_fusion
  102.2 2.3 %fusion.1 = f32[256,1152]{1,0:T(8,128)} fusion(f32[256,1152]{1,0:T(8,128)S(1)} %convolution_add_fusion.1, f32[256,1152]{1,0:T(8,128)S(1)} %collective-permute-done.2, f32[]{:T(128)} %bitcast, f32[256,256]{0,1:T(8,128)S(1)} %get-tuple-element.4), kind=kOutput, calls=%fused_computation.6 | convolution fusion | flops 906756096 | bytes 3801092 | tf_op jit(solution)/shard_map/dot_general | solution.py:34
  104.4 19.8 %collective-permute-done.6 = f32[256,1152]{1,0:T(8,128)S(1)} collective-permute-done((f32[256,1152]{1,0:T(8,128)S(1)}, f32[256,1152]{1,0:T(8,128)S(1)}, u32[]{:S(2)}, u32[]{:S(2)}) %collective-permute-start.6) | collective-permute-done | bytes 1179680 | tf_op jit(solution)/shard_map/ppermute | solution.py:12
  124.2 1.0 copy.10
  (2 shorter events, 0.0 us)
Async XLA Ops:
  0.6 6.0 %copy-start = (f32[256,1152]{1,0:T(8,128)S(1)}, f32[256,1152]{1,0:T(8,128)}, u32[]{:S(2)}) copy-start(f32[256,1152]{1,0:T(8,128)} %param.4) | copy-start | bytes 3538948
  0.6 18.1 %collective-permute-start = (f32[256,1152]{1,0:T(8,128)}, f32[256,1152]{1,0:T(8,128)S(1)}, u32[]{:S(2)}, u32[]{:S(2)}) collective-permute-start(f32[256,1152]{1,0:T(8,128)} %param.5), channel_id=1, source_target_pairs={{511,0},{0,1},{1,2},{2,3},{3,4},{4,5},{5,6},{6,7},{7,8},{8,9},{9,1... | collective-permute-start | bytes 3538952 | tf_op jit(solution)/shard_map/ppermute | solution.py:12
  10.6 20.7 %collective-permute-start.3 = (f32[256,1152]{1,0:T(8,128)S(1)}, f32[256,1152]{1,0:T(8,128)S(1)}, u32[]{:S(2)}, u32[]{:S(2)}) collective-permute-start(f32[256,1152]{1,0:T(8,128)S(1)} %convolution_multiply_fusion.3), channel_id=1, source_target_pairs={{511,0},{0,1},{1,2},{2,3},{3,4},{4,5},{5,6},{6,7},{7,8},{8,9},{9,1... | collective-permute-start | bytes 3538952 | tf_op jit(solution)/shard_map/ppermute | solution.py:12
  18.7 25.2 %collective-permute-start.1 = (f32[256,1152]{1,0:T(8,128)S(1)}, f32[256,1152]{1,0:T(8,128)S(1)}, u32[]{:S(2)}, u32[]{:S(2)}) collective-permute-start(f32[256,1152]{1,0:T(8,128)S(1)} %collective-permute-done), channel_id=1, source_target_pairs={{511,0},{0,1},{1,2},{2,3},{3,4},{4,5},{5,6},{6,7},{7,8},{8,9},{9,1... | collective-permute-start | bytes 3538952 | tf_op jit(solution)/shard_map/ppermute | solution.py:12
  32.6 24.0 %collective-permute-start.4 = (f32[256,1152]{1,0:T(8,128)S(1)}, f32[256,1152]{1,0:T(8,128)S(1)}, u32[]{:S(2)}, u32[]{:S(2)}) collective-permute-start(f32[256,1152]{1,0:T(8,128)S(1)} %fusion), channel_id=1, source_target_pairs={{511,0},{0,1},{1,2},{2,3},{3,4},{4,5},{5,6},{6,7},{7,8},{8,9},{9,1... | collective-permute-start | bytes 3538952 | tf_op jit(solution)/shard_map/ppermute | solution.py:12
  43.9 25.3 %collective-permute-start.2 = (f32[256,1152]{1,0:T(8,128)S(1)}, f32[256,1152]{1,0:T(8,128)S(1)}, u32[]{:S(2)}, u32[]{:S(2)}) collective-permute-start(f32[256,1152]{1,0:T(8,128)S(1)} %collective-permute-done.1), channel_id=1, source_target_pairs={{511,0},{0,1},{1,2},{2,3},{3,4},{4,5},{5,6},{6,7},{7,8},{8,9},{9,1... | collective-permute-start | bytes 3538952 | tf_op jit(solution)/shard_map/ppermute | solution.py:12
  51.0 10.3 %copy-start.1 = (f32[256,1152]{1,0:T(8,128)S(1)}, f32[256,1152]{1,0:T(8,128)}, u32[]{:S(2)}) copy-start(f32[256,1152]{1,0:T(8,128)} %param.5) | copy-start | bytes 3538948
  56.7 25.2 %collective-permute-start.5 = (f32[256,1152]{1,0:T(8,128)S(1)}, f32[256,1152]{1,0:T(8,128)S(1)}, u32[]{:S(2)}, u32[]{:S(2)}) collective-permute-start(f32[256,1152]{1,0:T(8,128)S(1)} %add.91), channel_id=1, source_target_pairs={{511,0},{0,1},{1,2},{2,3},{3,4},{4,5},{5,6},{6,7},{7,8},{8,9},{9,1... | collective-permute-start | bytes 3538952 | tf_op jit(solution)/shard_map/ppermute | solution.py:12
  82.0 42.2 %collective-permute-start.6 = (f32[256,1152]{1,0:T(8,128)S(1)}, f32[256,1152]{1,0:T(8,128)S(1)}, u32[]{:S(2)}, u32[]{:S(2)}) collective-permute-start(f32[256,1152]{1,0:T(8,128)S(1)} %add.92), channel_id=1, source_target_pairs={{3,0},{4,1},{5,2},{6,3},{7,4},{8,5},{9,6},{10,7},{11,8},{12,9},{13... | collective-permute-start | bytes 3538952 | tf_op jit(solution)/shard_map/ppermute | solution.py:12
where the time goes:
time: 126 us; the launch traced here: 125 us
  waiting for transfers between devices  61.9 us (49%)
  starting transfers between devices  41.2 us (33%)
  matrix products  18.2 us (14%)
  between operations  2.11 us (2%)
    ppermute x7, waiting for transfers between devices, from_behind(): return lax.ppermute(block, axis, route)  61.9 us
    ppermute x7, starting transfers between devices, from_behind(): return lax.ppermute(block, axis, route)  41.2 us
    dot_general x4, matrix products, pair_block(): lax.dot_general(images, partner, (((1,), (1,)), ((), ())), precision=high...  6.87 us
    dot_general x4, matrix products, pair_block(): img_part = temp * jnp.dot(coeff, partner, precision=highest)  6.13 us
    dot_general x4, matrix products, pair_block(): lax.dot_general(coeff, images, (((0,), (0,)), ((), ())), precision=highest)  5.16 us
  transfers between devices with their start and end apart: 7, of which 7 were waited for; matrix products, arithmetic and copies ran while one was open for 15% of the time, Pallas kernels for 0%

commit v1 on v0

v1 whole, which is shorter than its diff:
```python
import functools

import jax
import jax.numpy as jnp
from jax import lax
from jax.experimental import pallas as pl
from jax.experimental.pallas import tpu as pltpu
from jax.sharding import PartitionSpec as P

STEPS = 4
MESH = pl.DeviceIdType.MESH
F32 = jnp.float32
BF16 = jnp.bfloat16
CHUNKS = 2


def split(x):
    high = x.astype(BF16)
    return high, (x - high.astype(F32)).astype(BF16)


def dot3(a, b, dims):
    dot = functools.partial(
        lax.dot_general, dimension_numbers=(dims, ((), ())), preferred_element_type=F32
    )
    return dot(a[0], b[0]) + (dot(a[0], b[1]) + dot(a[1], b[0]))


def kernel(
    nx, ny, images, texts, log_temp, bias, row_loss, image_grad, text_grad,
    held, high, low, grad, loss, load_sem, send_sem, recv_sem,
):
    rows, width = images.shape
    part = rows // CHUNKS
    total = nx * ny
    me = lax.axis_index("gx") * ny + lax.axis_index("gy")
    core = lax.rem(me, 2)
    sign = 1 - 2 * core

    def at(p):
        p = lax.rem(p + total, total)
        return (p // ny, lax.rem(p, ny))

    mate, behind = at(me + sign), at(me - sign)
    ahead, back2 = at(me + 2 * sign), at(me - 2 * sign)

    loads = [
        pltpu.make_async_copy(texts, held.at[0, 0], load_sem.at[0]),
        pltpu.make_async_copy(images, held.at[1, 0], load_sem.at[1]),
    ]
    for load in loads:
        load.start()

    barrier = pltpu.get_barrier_semaphore()
    for device in (mate, behind, back2):
        pl.semaphore_signal(barrier, inc=1, device_id=device, device_id_type=MESH)
    for load in loads:
        load.wait()
    pl.semaphore_wait(barrier, 3)

    def copy(kind, stream, source, target, chunk, device):
        here = pl.ds(chunk * part, part)
        return pltpu.make_async_remote_copy(
            src_ref=held.at[stream, source, here],
            dst_ref=held.at[stream, target, here],
            send_sem=send_sem.at[kind, chunk],
            recv_sem=recv_sem.at[stream, target, chunk],
            device_id=device,
            device_id_type=MESH,
        )

    def own_to_next(chunk):
        return copy(0, 1 - core, 0, 1, chunk, behind)

    def own_to_ahead(chunk):
        return copy(1, core, 0, 2, chunk, ahead)

    def own_to_mate(chunk):
        return copy(2, core, 0, 1, chunk, mate)

    def pass_ahead(chunk):
        return copy(3, core, 1, 3, chunk, ahead)

    def relay_first(chunk):
        return copy(4, core, 1, 2, chunk, mate)

    def relay_second(chunk):
        return copy(5, core, 2, 3, chunk, mate)

    for chunk in range(CHUNKS):
        own_to_next(chunk).start()
    for chunk in range(CHUNKS):
        own_to_ahead(chunk).start()
    for chunk in range(CHUNKS):
        own_to_mate(chunk).start()

    for stream in range(2):
        high[stream], low[stream] = split(held[1 - stream, 0])
    grad[...] = jnp.zeros_like(grad)
    loss[...] = jnp.zeros_like(loss)
    temp = jnp.exp(jnp.full((1, part), log_temp[0], F32))
    shift = jnp.full((1, part), bias[0], F32)

    def unit(u, carry):
        block, chunk = u // CHUNKS, lax.rem(u, CHUNKS)
        slot = block // 2
        stream = lax.rem(core + 1 + block, 2)

        @pl.when(block >= 2)
        def _():
            here = pl.ds(chunk * part, part)
            pltpu.make_async_copy(
                held.at[stream, slot, here], held.at[stream, slot, here],
                recv_sem.at[stream, slot, chunk],
            ).wait()

        @pl.when(block == 3)
        def _():
            pass_ahead(chunk).start()
            relay_first(chunk).start()

        @pl.when(block == 5)
        def _():
            relay_second(chunk).start()

        start = pl.multiple_of(chunk * part, part)
        other = split(held[stream, slot, pl.ds(start, part), :])
        mine = (high[stream], low[stream])
        logits = temp * dot3(mine, other, ((1,), (1,))) + shift
        row = lax.broadcasted_iota(jnp.int32, (rows, part), 0)
        column = lax.broadcasted_iota(jnp.int32, (rows, part), 1)
        positive = jnp.logical_and(row == column + start, slot == 0)
        small = jnp.exp(-jnp.abs(logits))
        signed = jnp.where(positive, -logits, logits)
        loss[stream] += jnp.maximum(signed, 0.0) + jnp.log1p(small)
        sigmoid = jnp.where(logits >= 0, 1.0, small) / (1.0 + small)
        coeff = temp * jnp.where(positive, sigmoid - 1.0, sigmoid)
        grad[stream] += dot3(split(coeff), other, ((1,), (0,)))
        return carry

    lax.fori_loop(0, 2 * STEPS * CHUNKS, unit, 0)

    image_grad[...] = grad[0]
    text_grad[...] = grad[1]
    row_loss[...] = jnp.sum(loss[0].T, axis=0) / (STEPS * rows)
    for chunk in range(CHUNKS):
        for make in (own_to_next, own_to_ahead, own_to_mate, pass_ahead, relay_first, relay_second):
            make(chunk).wait_send()


def solution(mesh):
    nx, ny = mesh.shape["gx"], mesh.shape["gy"]

    def per_device(images, texts, log_temp, bias):
        rows, width = images.shape
        part = rows // CHUNKS
        vmem = pl.BlockSpec(memory_space=pltpu.VMEM)
        smem = pl.BlockSpec(memory_space=pltpu.SMEM)
        hbm = pl.BlockSpec(memory_space=pl.ANY)
        return pl.pallas_call(
            functools.partial(kernel, nx, ny),
            out_shape=(
                jax.ShapeDtypeStruct((rows,), F32),
                jax.ShapeDtypeStruct((rows, width), F32),
                jax.ShapeDtypeStruct((rows, width), F32),
            ),
            in_specs=[hbm, hbm, smem, smem],
            out_specs=(vmem, vmem, vmem),
            scratch_shapes=[
                pltpu.VMEM((2, STEPS, rows, width), F32),
                pltpu.VMEM((2, rows, width), BF16),
                pltpu.VMEM((2, rows, width), BF16),
                pltpu.VMEM((2, rows, width), F32),
                pltpu.VMEM((2, rows, part), F32),
                pltpu.SemaphoreType.DMA((2,)),
                pltpu.SemaphoreType.DMA((6, CHUNKS)),
                pltpu.SemaphoreType.DMA((2, STEPS, CHUNKS)),
            ],
            compiler_params=pltpu.CompilerParams(
                collective_id=0, has_side_effects=True, vmem_limit_bytes=48 << 20
            ),
        )(images, texts, log_temp, bias)

    return jax.shard_map(
        per_device,
        mesh=mesh,
        in_specs=(P(("gx", "gy"), None), P(("gx", "gy"), None), P(), P()),
        out_specs=(P(("gx", "gy")), P(("gx", "gy"), None), P(("gx", "gy"), None)),
        check_vma=False,
    )
```

time: 126 us -> 66.5 us (0.53)
  waiting for transfers between devices: 61.9 us -> 0 us
  Pallas kernels: 0 us -> 58.8 us
  starting transfers between devices: 41.2 us -> 0 us
  matrix products: 18.2 us -> 0 us
  local copies, waits for them, and re-layouts: 1.03 us -> 5.12 us
    ppermute x7 -> x0, waiting for transfers between devices: 61.9 us -> none  [from_behind(): return lax.ppermute(block, axis, route)]
    pallas_call x0 -> x1, Pallas kernels: none -> 58.8 us  [per_device(): pl.pallas_call(functools.partial(kernel, nx, ny), out_shape=(jax.ShapeDty...]
    ppermute x7 -> x0, starting transfers between devices: 41.2 us -> none  [from_behind(): return lax.ppermute(block, axis, route)]
    dot_general x12 -> x0, matrix products: 18.2 us -> none  [the longest x4 6.87 us: pair_block(): lax.dot_general(images, partner, (((1,), (1,)), ((), ())), precision=high...]
    unnamed x5 -> x7, local copies, waits for them, and re-layouts: 1.03 us -> 5.12 us
  transfers between devices with their start and end apart: 7 -> 0, of which waited for: 7 -> 0; matrix products, arithmetic and copies ran while one was open for 15% -> 0% of each run, Pallas kernels for 0% -> 0%
where the time goes in v1:
time: 66.5 us; the launch traced here: 65.8 us
  Pallas kernels  58.8 us (88%)
  local copies, waits for them, and re-layouts  5.12 us (8%)
  between operations  1.94 us (3%)
    pallas_call x1, Pallas kernels, per_device(): pl.pallas_call(functools.partial(kernel, nx, ny), out_shape=(jax.ShapeDty...  58.8 us
    unnamed x7, local copies, waits for them, and re-layouts  5.12 us

profile of v1, /device:TPU:1, one launch (start us, length us, event | category | flops | bytes accessed | tf_op | source)
XLA Modules:
  0.0 65.8 jit_solution(5889841065626717579)
XLA Ops:
  1.9 0.0 copy-start
  1.9 1.3 %copy-done = f32[256,1152]{1,0:T(8,128)S(1)} copy-done((f32[256,1152]{1,0:T(8,128)S(1)}, f32[256,1152]{1,0:T(8,128)}, u32[]{:S(2)}) %copy-start) | copy-done | bytes 1179672
  3.2 0.0 copy-start.1
  3.2 1.3 %copy-done.1 = f32[256,1152]{1,0:T(8,128)S(1)} copy-done((f32[256,1152]{1,0:T(8,128)S(1)}, f32[256,1152]{1,0:T(8,128)}, u32[]{:S(2)}) %copy-start.1) | copy-done | bytes 1179672
  4.5 58.8 %shard_map.67 = (f32[256]{0:T(256)S(1)}, f32[256,1152]{1,0:T(8,128)S(1)}, f32[256,1152]{1,0:T(8,128)S(1)}) custom-call(f32[256,1152]{1,0:T(8,128)S(1)} %copy-done, f32[256,1152]{1,0:T(8,128)S(1)} %copy-done.1, f32[1]{0:T(128)S(6)} %copy.10.log_temp, f32[1]{0:T(128)S(6)} %copy.11.bias), custom_call_target="tpu_custom_call" | custom-call | tf_op jit(solution)/shard_map/pallas_call | solution.py:160
  63.2 0.6 copy.12
  63.8 1.0 %copy.13 = f32[256,1152]{1,0:T(8,128)} copy(f32[256,1152]{1,0:T(8,128)S(1)} %get-tuple-element.7) | data formatting | bytes 2359296
  64.8 1.0 %copy.14 = f32[256,1152]{1,0:T(8,128)} copy(f32[256,1152]{1,0:T(8,128)S(1)} %get-tuple-element.8) | data formatting | bytes 2359296
Async XLA Ops:
  1.9 1.3 %copy-start = (f32[256,1152]{1,0:T(8,128)S(1)}, f32[256,1152]{1,0:T(8,128)}, u32[]{:S(2)}) copy-start(f32[256,1152]{1,0:T(8,128)} %images.1) | copy-start | bytes 3538948
  3.2 1.3 %copy-start.1 = (f32[256,1152]{1,0:T(8,128)S(1)}, f32[256,1152]{1,0:T(8,128)}, u32[]{:S(2)}) copy-start(f32[256,1152]{1,0:T(8,128)} %texts.1) | copy-start | bytes 3538948

commit v2 on v1

v2 whole, which is shorter than its diff:
```python
import functools

import jax
import jax.numpy as jnp
from jax import lax
from jax.experimental import pallas as pl
from jax.experimental.pallas import tpu as pltpu
from jax.sharding import PartitionSpec as P

STEPS = 4
MESH = pl.DeviceIdType.MESH
F32 = jnp.float32
BF16 = jnp.bfloat16
CHUNKS = 2
NT = ((1,), (1,))
NN = ((1,), (0,))


def split(x):
    high = x.astype(BF16)
    return high, (x - high.astype(F32)).astype(BF16)


def dot(a, b, dims):
    return lax.dot_general(a, b, (dims, ((), ())), preferred_element_type=F32)


def dot3(a, b, dims):
    return dot(a[0], b[0], dims) + (dot(a[0], b[1], dims) + dot(a[1], b[0], dims))


def kernel(
    nx, ny, images, texts, scalars, row_loss, image_grad, text_grad,
    held, high, low, grad, loss, load_sem, send_sem, recv_sem,
):
    rows, width = images.shape
    part = rows // CHUNKS
    total = nx * ny
    me = lax.axis_index("gx") * ny + lax.axis_index("gy")
    core = lax.rem(me, 2)
    sign = 1 - 2 * core

    def at(p):
        p = lax.rem(p + total, total)
        return (p // ny, lax.rem(p, ny))

    mate, behind = at(me + sign), at(me - sign)
    ahead, back2 = at(me + 2 * sign), at(me - 2 * sign)

    loads = [
        pltpu.make_async_copy(texts, held.at[0, 0], load_sem.at[0]),
        pltpu.make_async_copy(images, held.at[1, 0], load_sem.at[1]),
    ]
    for load in loads:
        load.start()

    barrier = pltpu.get_barrier_semaphore()
    for device in (mate, behind, back2):
        pl.semaphore_signal(barrier, inc=1, device_id=device, device_id_type=MESH)
    pl.semaphore_wait(barrier, 3)

    def copy(kind, stream, source, target, chunk, device):
        here = pl.ds(chunk * part, part)
        if source is None:
            source = held.at[stream, target - 1]
        return pltpu.make_async_remote_copy(
            src_ref=source.at[here],
            dst_ref=held.at[stream, target, here],
            send_sem=send_sem.at[kind, chunk],
            recv_sem=recv_sem.at[stream, target, chunk],
            device_id=device,
            device_id_type=MESH,
        )

    def own_to_next(chunk, mine, other):
        return copy(0, 1 - core, other, 1, chunk, behind)

    def own_to_ahead(chunk, mine, other):
        return copy(1, core, mine, 2, chunk, ahead)

    def own_to_mate(chunk, mine, other):
        return copy(2, core, mine, 1, chunk, mate)

    def pass_ahead(chunk):
        return copy(3, core, held.at[core, 1], 3, chunk, ahead)

    def relay_first(chunk):
        return copy(4, core, held.at[core, 1], 2, chunk, mate)

    def relay_second(chunk):
        return copy(5, core, held.at[core, 2], 3, chunk, mate)

    for which, mine, other in ((0, texts, images), (1, images, texts)):

        @pl.when(core == which)
        def _():
            for make in (own_to_next, own_to_ahead, own_to_mate):
                for chunk in range(CHUNKS):
                    make(chunk, mine, other).start()

    for load in loads:
        load.wait()
    for stream in range(2):
        high[stream], low[stream] = split(held[1 - stream, 0])
    grad[...] = jnp.zeros_like(grad)
    loss[...] = jnp.zeros_like(loss)
    temp = jnp.exp(scalars[0:1, :])
    shift = scalars[1:2, :]

    def arrived(stream, slot, chunk):
        here = held.at[stream, slot, pl.ds(chunk * part, part)]
        pltpu.make_async_copy(here, here, recv_sem.at[stream, slot, chunk]).wait()

    def coefficients(logits, positive):
        logits = temp * logits + shift
        small = jnp.exp(-jnp.abs(logits))
        sigmoid = jnp.where(logits >= 0, 1.0, small) / (1.0 + small)
        if positive is None:
            return jnp.maximum(logits, 0.0) + jnp.log1p(small), temp * sigmoid
        signed = jnp.where(positive, -logits, logits)
        losses = jnp.maximum(signed, 0.0) + jnp.log1p(small)
        return losses, temp * jnp.where(positive, sigmoid - 1.0, sigmoid)

    def whole(block, carry):
        slot = block // 2
        stream = lax.rem(core + 1 + block, 2)
        for chunk in range(CHUNKS):

            @pl.when(block >= 2)
            def _():
                arrived(stream, slot, chunk)

            @pl.when(block == 3)
            def _():
                pass_ahead(chunk).start()
                relay_first(chunk).start()

            @pl.when(block == 5)
            def _():
                relay_second(chunk).start()

        other = split(held[stream, slot])
        logits = dot3((high[stream], low[stream]), other, NT)
        pieces = []
        for chunk in range(CHUNKS):
            here = slice(chunk * part, (chunk + 1) * part)
            row = lax.broadcasted_iota(jnp.int32, (rows, part), 0)
            column = lax.broadcasted_iota(jnp.int32, (rows, part), 1) + chunk * part
            positive = jnp.logical_and(row == column, slot == 0)
            losses, coeff = coefficients(logits[:, here], positive)
            loss[stream] += losses
            pieces.append(coeff)
        grad[stream] += dot3(split(jnp.concatenate(pieces, axis=1)), other, NN)
        return carry

    def last(chunk, carry):
        arrived(core, STEPS - 1, chunk)
        start = pl.multiple_of(chunk * part, part)
        far, near = split(held[core, STEPS - 1, pl.ds(start, part), :])
        both = dot(high[core], jnp.concatenate([far, near], axis=0), NT)
        logits = both[:, :part] + both[:, part:] + dot(low[core], far, NT)
        losses, coeff = coefficients(logits, None)
        loss[core] += losses
        top, rest = split(coeff)
        grad[core] += dot(
            jnp.concatenate([top, rest], axis=1), jnp.concatenate([far, far], axis=0), NN
        ) + dot(top, near, NN)
        return carry

    lax.fori_loop(0, 2 * STEPS - 1, whole, 0)
    lax.fori_loop(0, CHUNKS, last, 0)

    image_grad[...] = grad[0]
    text_grad[...] = grad[1]
    row_loss[...] = jnp.sum(loss[0].T, axis=0) / (STEPS * rows)
    for chunk in range(CHUNKS):
        for make in (own_to_next, own_to_ahead, own_to_mate):
            make(chunk, texts, texts).wait_send()
        for make in (pass_ahead, relay_first, relay_second):
            make(chunk).wait_send()


def solution(mesh):
    nx, ny = mesh.shape["gx"], mesh.shape["gy"]

    def per_device(images, texts, log_temp, bias):
        rows, width = images.shape
        part = rows // CHUNKS
        vmem = pl.BlockSpec(memory_space=pltpu.VMEM)
        hbm = pl.BlockSpec(memory_space=pltpu.HBM)
        return pl.pallas_call(
            functools.partial(kernel, nx, ny),
            out_shape=(
                jax.ShapeDtypeStruct((rows,), F32),
                jax.ShapeDtypeStruct((rows, width), F32),
                jax.ShapeDtypeStruct((rows, width), F32),
            ),
            in_specs=[hbm, hbm, vmem],
            out_specs=(vmem, vmem, vmem),
            scratch_shapes=[
                pltpu.VMEM((2, STEPS, rows, width), F32),
                pltpu.VMEM((2, rows, width), BF16),
                pltpu.VMEM((2, rows, width), BF16),
                pltpu.VMEM((2, rows, width), F32),
                pltpu.VMEM((2, rows, part), F32),
                pltpu.SemaphoreType.DMA((2,)),
                pltpu.SemaphoreType.DMA((6, CHUNKS)),
                pltpu.SemaphoreType.DMA((2, STEPS, CHUNKS)),
            ],
            compiler_params=pltpu.CompilerParams(
                collective_id=0, has_side_effects=True, vmem_limit_bytes=51 << 20
            ),
        )(images, texts, jnp.stack([jnp.broadcast_to(log_temp, (part,)), jnp.broadcast_to(bias, (part,))]))

    return jax.shard_map(
        per_device,
        mesh=mesh,
        in_specs=(P(("gx", "gy"), None), P(("gx", "gy"), None), P(), P()),
        out_specs=(P(("gx", "gy")), P(("gx", "gy"), None), P(("gx", "gy"), None)),
        check_vma=False,
    )
```

time: 66.5 us -> 60.3 us (0.907)
  Pallas kernels: 58.8 us -> 55.3 us
  local copies, waits for them, and re-layouts: 5.12 us -> 2.66 us
    pallas_call x1, Pallas kernels: 58.8 us -> 55.3 us  [per_device(): pl.pallas_call(functools.partial(kernel, nx, ny), out_shape=(jax.ShapeDty...]
    unnamed x7 -> x3, local copies, waits for them, and re-layouts: 5.12 us -> 2.59 us
where the time goes in v2:
time: 60.3 us; the launch traced here: 59.9 us
  Pallas kernels  55.3 us (92%)
  local copies, waits for them, and re-layouts  2.66 us (4%)
  between operations  1.94 us (3%)
    pallas_call x1, Pallas kernels, per_device(): pl.pallas_call(functools.partial(kernel, nx, ny), out_shape=(jax.ShapeDty...  55.3 us
    unnamed x3, local copies, waits for them, and re-layouts  2.59 us

profile of v2, /device:TPU:1, one launch (start us, length us, event | category | flops | bytes accessed | tf_op | source)
XLA Modules:
  0.0 59.9 jit_solution(1780213365915005976)
XLA Ops:
  1.9 0.1 stack.6.scalars
  2.0 55.3 %shard_map.70 = (f32[256]{0:T(256)S(1)}, f32[256,1152]{1,0:T(8,128)S(1)}, f32[256,1152]{1,0:T(8,128)S(1)}) custom-call(f32[256,1152]{1,0:T(8,128)} %images.1, f32[256,1152]{1,0:T(8,128)} %texts.1, f32[2,128]{1,0:T(2,128)S(1)} %stack.6.scalars), custom_call_target="tpu_custom_call" | custom-call | tf_op jit(solution)/shard_map/pallas_call | solution.py:191
  57.3 0.6 copy.12
  57.9 1.0 %copy.13 = f32[256,1152]{1,0:T(8,128)} copy(f32[256,1152]{1,0:T(8,128)S(1)} %get-tuple-element.7) | data formatting | bytes 2359296
  58.9 1.0 %copy.14 = f32[256,1152]{1,0:T(8,128)} copy(f32[256,1152]{1,0:T(8,128)S(1)} %get-tuple-element.8) | data formatting | bytes 2359296
  (1 shorter events, 0.0 us)

commit v3 on v2

--- a/solution.py
+++ b/solution.py
@@ -180,6 +180,18 @@
             make(chunk).wait_send()
 
 
+def finish(losses, first, second, row_loss, image_grad, text_grad, sem):
+    copies = [
+        pltpu.make_async_copy(first, image_grad, sem.at[0]),
+        pltpu.make_async_copy(second, text_grad, sem.at[1]),
+        pltpu.make_async_copy(losses, row_loss, sem.at[2]),
+    ]
+    for copy in copies:
+        copy.start()
+    for copy in copies:
+        copy.wait()
+
+
 def solution(mesh):
     nx, ny = mesh.shape["gx"], mesh.shape["gy"]
 
@@ -188,13 +200,14 @@
         part = rows // CHUNKS
         vmem = pl.BlockSpec(memory_space=pltpu.VMEM)
         hbm = pl.BlockSpec(memory_space=pltpu.HBM)
-        return pl.pallas_call(
+        shapes = (
+            jax.ShapeDtypeStruct((rows,), F32),
+            jax.ShapeDtypeStruct((rows, width), F32),
+            jax.ShapeDtypeStruct((rows, width), F32),
+        )
+        results = pl.pallas_call(
             functools.partial(kernel, nx, ny),
-            out_shape=(
-                jax.ShapeDtypeStruct((rows,), F32),
-                jax.ShapeDtypeStruct((rows, width), F32),
-                jax.ShapeDtypeStruct((rows, width), F32),
-            ),
+            out_shape=shapes,
             in_specs=[hbm, hbm, vmem],
             out_specs=(vmem, vmem, vmem),
             scratch_shapes=[
@@ -211,6 +224,14 @@
                 collective_id=0, has_side_effects=True, vmem_limit_bytes=51 << 20
             ),
         )(images, texts, jnp.stack([jnp.broadcast_to(log_temp, (part,)), jnp.broadcast_to(bias, (part,))]))
+        return pl.pallas_call(
+            finish,
+            out_shape=shapes,
+            in_specs=[vmem] * 3,
+            out_specs=(hbm, hbm, hbm),
+            scratch_shapes=[pltpu.SemaphoreType.DMA((3,))],
+            compiler_params=pltpu.CompilerParams(vmem_limit_bytes=8 << 20),
+        )(*results)
 
     return jax.shard_map(
         per_device,

time: 60.3 us -> 59.1 us (0.980)
  local copies, waits for them, and re-layouts: 2.66 us -> 0.07 us
  Pallas kernels: 55.3 us -> 56.7 us
    unnamed x3 -> x0, local copies, waits for them, and re-layouts: 2.59 us -> none
    pallas_call x1 -> x2, Pallas kernels: 55.3 us -> 56.7 us  [the longest x1 55.3 us: per_device(): pl.pallas_call(functools.partial(kernel, nx, ny), out_shape=shapes, in_sp...]
where the time goes in v3:
time: 59.1 us; the launch traced here: 58.7 us
  Pallas kernels  56.7 us (96%)
  between operations  1.94 us (3%)
    pallas_call x1, Pallas kernels, per_device(): pl.pallas_call(functools.partial(kernel, nx, ny), out_shape=shapes, in_sp...  55.3 us
    pallas_call x1, Pallas kernels, per_device(): pl.pallas_call(finish, out_shape=shapes, in_specs=[vmem] * 3, out_specs=(...  1.43 us

profile of v3, /device:TPU:1, one launch (start us, length us, event | category | flops | bytes accessed | tf_op | source)
XLA Modules:
  0.0 58.7 jit_solution(12791584643292738480)
XLA Ops:
  1.9 0.1 stack.6.scalars
  2.0 55.3 %shard_map.70 = (f32[256]{0:T(256)S(1)}, f32[256,1152]{1,0:T(8,128)S(1)}, f32[256,1152]{1,0:T(8,128)S(1)}) custom-call(f32[256,1152]{1,0:T(8,128)} %images.1, f32[256,1152]{1,0:T(8,128)} %texts.1, f32[2,128]{1,0:T(2,128)S(1)} %stack.6.scalars), custom_call_target="tpu_custom_call" | custom-call | tf_op jit(solution)/shard_map/pallas_call | solution.py:208
  57.3 1.4 %shard_map.71 = (f32[256]{0:T(256)}, f32[256,1152]{1,0:T(8,128)}, f32[256,1152]{1,0:T(8,128)}) custom-call(f32[256]{0:T(256)S(1)} %get-tuple-element.6.losses, f32[256,1152]{1,0:T(8,128)S(1)} %get-tuple-element.7.first, f32[256,1152]{1,0:T(8,128)S(1)} %get-tuple-element.8.second), custom_call_target="tpu_custom_call" | custom-call | tf_op jit(solution)/shard_map/pallas_call | solution.py:227
  (1 shorter events, 0.0 us)

commit v4 on v3

--- a/solution.py
+++ b/solution.py
@@ -12,6 +12,7 @@
 F32 = jnp.float32
 BF16 = jnp.bfloat16
 CHUNKS = 2
+TAIL = 4
 NT = ((1,), (1,))
 NN = ((1,), (0,))
 
@@ -59,8 +60,8 @@
         pl.semaphore_signal(barrier, inc=1, device_id=device, device_id_type=MESH)
     pl.semaphore_wait(barrier, 3)
 
-    def copy(kind, stream, source, target, chunk, device):
-        here = pl.ds(chunk * part, part)
+    def copy(kind, stream, source, target, chunk, device, size=part):
+        here = pl.ds(chunk * size, size)
         if source is None:
             source = held.at[stream, target - 1]
         return pltpu.make_async_remote_copy(
@@ -82,7 +83,7 @@
         return copy(2, core, mine, 1, chunk, mate)
 
     def pass_ahead(chunk):
-        return copy(3, core, held.at[core, 1], 3, chunk, ahead)
+        return copy(3, core, held.at[core, 1], 3, chunk, ahead, rows // TAIL)
 
     def relay_first(chunk):
         return copy(4, core, held.at[core, 1], 2, chunk, mate)
@@ -107,16 +108,17 @@
     temp = jnp.exp(scalars[0:1, :])
     shift = scalars[1:2, :]
 
-    def arrived(stream, slot, chunk):
-        here = held.at[stream, slot, pl.ds(chunk * part, part)]
+    def arrived(stream, slot, chunk, size=part):
+        here = held.at[stream, slot, pl.ds(chunk * size, size)]
         pltpu.make_async_copy(here, here, recv_sem.at[stream, slot, chunk]).wait()
 
     def coefficients(logits, positive):
-        logits = temp * logits + shift
+        wide = logits.shape[1]
+        logits = temp[:, :wide] * logits + shift[:, :wide]
         small = jnp.exp(-jnp.abs(logits))
         sigmoid = jnp.where(logits >= 0, 1.0, small) / (1.0 + small)
         if positive is None:
-            return jnp.maximum(logits, 0.0) + jnp.log1p(small), temp * sigmoid
+            return jnp.maximum(logits, 0.0) + jnp.log1p(small), temp[:, :wide] * sigmoid
         signed = jnp.where(positive, -logits, logits)
         losses = jnp.maximum(signed, 0.0) + jnp.log1p(small)
         return losses, temp * jnp.where(positive, sigmoid - 1.0, sigmoid)
@@ -132,7 +134,8 @@
 
             @pl.when(block == 3)
             def _():
-                pass_ahead(chunk).start()
+                for piece in range(TAIL // CHUNKS):
+                    pass_ahead(chunk * (TAIL // CHUNKS) + piece).start()
                 relay_first(chunk).start()
 
             @pl.when(block == 5)
@@ -153,22 +156,25 @@
         grad[stream] += dot3(split(jnp.concatenate(pieces, axis=1)), other, NN)
         return carry
 
-    def last(chunk, carry):
-        arrived(core, STEPS - 1, chunk)
-        start = pl.multiple_of(chunk * part, part)
-        far, near = split(held[core, STEPS - 1, pl.ds(start, part), :])
+    def last(piece, carry):
+        size = rows // TAIL
+        arrived(core, STEPS - 1, piece, size)
+        start = pl.multiple_of(piece * size, size)
+        far, near = split(held[core, STEPS - 1, pl.ds(start, size), :])
         both = dot(high[core], jnp.concatenate([far, near], axis=0), NT)
-        logits = both[:, :part] + both[:, part:] + dot(low[core], far, NT)
+        logits = both[:, :size] + both[:, size:] + dot(low[core], far, NT)
         losses, coeff = coefficients(logits, None)
-        loss[core] += losses
+        loss[core, :, :size] += losses
         top, rest = split(coeff)
         grad[core] += dot(
-            jnp.concatenate([top, rest], axis=1), jnp.concatenate([far, far], axis=0), NN
-        ) + dot(top, near, NN)
+            jnp.concatenate([top, rest, top], axis=1),
+            jnp.concatenate([far, far, near], axis=0),
+            NN,
+        )
         return carry
 
     lax.fori_loop(0, 2 * STEPS - 1, whole, 0)
-    lax.fori_loop(0, CHUNKS, last, 0)
+    lax.fori_loop(0, TAIL, last, 0)
 
     image_grad[...] = grad[0]
     text_grad[...] = grad[1]
@@ -176,8 +182,10 @@
     for chunk in range(CHUNKS):
         for make in (own_to_next, own_to_ahead, own_to_mate):
             make(chunk, texts, texts).wait_send()
-        for make in (pass_ahead, relay_first, relay_second):
+        for make in (relay_first, relay_second):
             make(chunk).wait_send()
+    for piece in range(TAIL):
+        pass_ahead(piece).wait_send()
 
 
 def finish(losses, first, second, row_loss, image_grad, text_grad, sem):
@@ -217,8 +225,8 @@
                 pltpu.VMEM((2, rows, width), F32),
                 pltpu.VMEM((2, rows, part), F32),
                 pltpu.SemaphoreType.DMA((2,)),
-                pltpu.SemaphoreType.DMA((6, CHUNKS)),
-                pltpu.SemaphoreType.DMA((2, STEPS, CHUNKS)),
+                pltpu.SemaphoreType.DMA((6, TAIL)),
+                pltpu.SemaphoreType.DMA((2, STEPS, TAIL)),
             ],
             compiler_params=pltpu.CompilerParams(
                 collective_id=0, has_side_effects=True, vmem_limit_bytes=51 << 20

time: 59.1 us -> 60.6 us (1.025)
  Pallas kernels: 56.7 us -> 58.4 us
    pallas_call x1, Pallas kernels: 55.3 us -> 57 us  [per_device(): pl.pallas_call(functools.partial(kernel, nx, ny), out_shape=shapes, in_sp...]
where the time goes in v4:
time: 60.6 us; the launch traced here: 60.5 us
  Pallas kernels  58.4 us (96%)
  between operations  1.94 us (3%)
    pallas_call x1, Pallas kernels, per_device(): pl.pallas_call(functools.partial(kernel, nx, ny), out_shape=shapes, in_sp...  57 us
    pallas_call x1, Pallas kernels, per_device(): pl.pallas_call(finish, out_shape=shapes, in_specs=[vmem] * 3, out_specs=(...  1.43 us

profile of v4, /device:TPU:1, one launch (start us, length us, event | category | flops | bytes accessed | tf_op | source)
XLA Modules:
  0.0 60.5 jit_solution(8618812190613400279)
XLA Ops:
  1.9 0.1 stack.6.scalars
  2.0 57.0 %shard_map.70 = (f32[256]{0:T(256)S(1)}, f32[256,1152]{1,0:T(8,128)S(1)}, f32[256,1152]{1,0:T(8,128)S(1)}) custom-call(f32[256,1152]{1,0:T(8,128)} %images.1, f32[256,1152]{1,0:T(8,128)} %texts.1, f32[2,128]{1,0:T(2,128)S(1)} %stack.6.scalars), custom_call_target="tpu_custom_call" | custom-call | tf_op jit(solution)/shard_map/pallas_call | solution.py:216
  59.0 1.4 %shard_map.71 = (f32[256]{0:T(256)}, f32[256,1152]{1,0:T(8,128)}, f32[256,1152]{1,0:T(8,128)}) custom-call(f32[256]{0:T(256)S(1)} %get-tuple-element.6.losses, f32[256,1152]{1,0:T(8,128)S(1)} %get-tuple-element.7.first, f32[256,1152]{1,0:T(8,128)S(1)} %get-tuple-element.8.second), custom_call_target="tpu_custom_call" | custom-call | tf_op jit(solution)/shard_map/pallas_call | solution.py:235
  (1 shorter events, 0.0 us)

commit v5 on v3

--- a/solution.py
+++ b/solution.py
@@ -12,6 +12,7 @@
 F32 = jnp.float32
 BF16 = jnp.bfloat16
 CHUNKS = 2
+PIECES = 4
 NT = ((1,), (1,))
 NN = ((1,), (0,))
 
@@ -167,11 +168,18 @@
         ) + dot(top, near, NN)
         return carry
 
+    def hand_over(which, stream, result):
+        @pl.when(which == stream)
+        def _():
+            result[...] = grad[stream]
+
     lax.fori_loop(0, 2 * STEPS - 1, whole, 0)
+    hand_over(1 - core, 0, image_grad)
+    hand_over(1 - core, 1, text_grad)
     lax.fori_loop(0, CHUNKS, last, 0)
-
-    image_grad[...] = grad[0]
-    text_grad[...] = grad[1]
+    hand_over(core, 0, image_grad)
+    hand_over(core, 1, text_grad)
+
     row_loss[...] = jnp.sum(loss[0].T, axis=0) / (STEPS * rows)
     for chunk in range(CHUNKS):
         for make in (own_to_next, own_to_ahead, own_to_mate):
@@ -181,11 +189,14 @@
 
 
 def finish(losses, first, second, row_loss, image_grad, text_grad, sem):
-    copies = [
-        pltpu.make_async_copy(first, image_grad, sem.at[0]),
-        pltpu.make_async_copy(second, text_grad, sem.at[1]),
-        pltpu.make_async_copy(losses, row_loss, sem.at[2]),
-    ]
+    size = first.shape[0] // PIECES
+    copies = [pltpu.make_async_copy(losses, row_loss, sem.at[0, PIECES])]
+    for piece in range(PIECES):
+        here = pl.ds(piece * size, size)
+        copies += [
+            pltpu.make_async_copy(first.at[here], image_grad.at[here], sem.at[0, piece]),
+            pltpu.make_async_copy(second.at[here], text_grad.at[here], sem.at[1, piece]),
+        ]
     for copy in copies:
         copy.start()
     for copy in copies:
@@ -229,7 +240,7 @@
             out_shape=shapes,
             in_specs=[vmem] * 3,
             out_specs=(hbm, hbm, hbm),
-            scratch_shapes=[pltpu.SemaphoreType.DMA((3,))],
+            scratch_shapes=[pltpu.SemaphoreType.DMA((2, PIECES + 1))],
             compiler_params=pltpu.CompilerParams(vmem_limit_bytes=8 << 20),
         )(*results)
 

time: 59.1 us -> 59.2 us (level)
  no operation moved by 1% of the time
where the time goes in v5:
time: 59.2 us; the launch traced here: 58.9 us
  Pallas kernels  56.9 us (96%)
  between operations  1.94 us (3%)
    pallas_call x1, Pallas kernels, per_device(): pl.pallas_call(functools.partial(kernel, nx, ny), out_shape=shapes, in_sp...  55.4 us
    pallas_call x1, Pallas kernels, per_device(): pl.pallas_call(finish, out_shape=shapes, in_specs=[vmem] * 3, out_specs=(...  1.49 us

profile of v5, /device:TPU:1, one launch (start us, length us, event | category | flops | bytes accessed | tf_op | source)
XLA Modules:
  0.0 58.9 jit_solution(4083256307586185301)
XLA Ops:
  1.9 0.1 stack.6.scalars
  2.0 55.4 %shard_map.70 = (f32[256]{0:T(256)S(1)}, f32[256,1152]{1,0:T(8,128)S(1)}, f32[256,1152]{1,0:T(8,128)S(1)}) custom-call(f32[256,1152]{1,0:T(8,128)} %images.1, f32[256,1152]{1,0:T(8,128)} %texts.1, f32[2,128]{1,0:T(2,128)S(1)} %stack.6.scalars), custom_call_target="tpu_custom_call" | custom-call | tf_op jit(solution)/shard_map/pallas_call | solution.py:219
  57.4 1.5 %shard_map.71 = (f32[256]{0:T(256)}, f32[256,1152]{1,0:T(8,128)}, f32[256,1152]{1,0:T(8,128)}) custom-call(f32[256]{0:T(256)S(1)} %get-tuple-element.6.losses, f32[256,1152]{1,0:T(8,128)S(1)} %get-tuple-element.7.first, f32[256,1152]{1,0:T(8,128)S(1)} %get-tuple-element.8.second), custom_call_target="tpu_custom_call" | custom-call | tf_op jit(solution)/shard_map/pallas_call | solution.py:238
  (1 shorter events, 0.0 us)

commit v6 on v5

--- a/solution.py
+++ b/solution.py
@@ -95,7 +95,7 @@
 
         @pl.when(core == which)
         def _():
-            for make in (own_to_next, own_to_ahead, own_to_mate):
+            for make in (own_to_mate, own_to_next, own_to_ahead):
                 for chunk in range(CHUNKS):
                     make(chunk, mine, other).start()
 

time: 59.2 us -> 59.2 us (level)
  no operation moved by 1% of the time
where the time goes in v6:
time: 59.2 us; the launch traced here: 58.9 us
  Pallas kernels  56.9 us (96%)
  between operations  1.94 us (3%)
    pallas_call x1, Pallas kernels, per_device(): pl.pallas_call(functools.partial(kernel, nx, ny), out_shape=shapes, in_sp...  55.4 us
    pallas_call x1, Pallas kernels, per_device(): pl.pallas_call(finish, out_shape=shapes, in_specs=[vmem] * 3, out_specs=(...  1.49 us

profile of v6, /device:TPU:1, one launch (start us, length us, event | category | flops | bytes accessed | tf_op | source)
XLA Modules:
  0.0 58.9 jit_solution(1942978968683439446)
XLA Ops:
  1.9 0.1 stack.6.scalars
  2.0 55.4 %shard_map.70 = (f32[256]{0:T(256)S(1)}, f32[256,1152]{1,0:T(8,128)S(1)}, f32[256,1152]{1,0:T(8,128)S(1)}) custom-call(f32[256,1152]{1,0:T(8,128)} %images.1, f32[256,1152]{1,0:T(8,128)} %texts.1, f32[2,128]{1,0:T(2,128)S(1)} %stack.6.scalars), custom_call_target="tpu_custom_call" | custom-call | tf_op jit(solution)/shard_map/pallas_call | solution.py:219
  57.4 1.5 %shard_map.71 = (f32[256]{0:T(256)}, f32[256,1152]{1,0:T(8,128)}, f32[256,1152]{1,0:T(8,128)}) custom-call(f32[256]{0:T(256)S(1)} %get-tuple-element.6.losses, f32[256,1152]{1,0:T(8,128)S(1)} %get-tuple-element.7.first, f32[256,1152]{1,0:T(8,128)S(1)} %get-tuple-element.8.second), custom_call_target="tpu_custom_call" | custom-call | tf_op jit(solution)/shard_map/pallas_call | solution.py:238
  (1 shorter events, 0.0 us)
